TPU v7x, 256 devices: a whole 4x4x8 slice. The times are simulated.
256 devices in a mesh: fsdp: 32 (over y, x, core), ctx: 8 (over z).
Axes of the slice: x: 4, y: 4, z: 8, core: 2. Of those that a mesh axis runs over, the one named last changes fastest.
Arguments:
- tokens: bfloat16 [16384, 8192], P('fsdp'), may hold values from -12 to 12
- wq: bfloat16 [8192, 4096], P('fsdp', 'ctx'), may hold values from -0.0625 to 0.0625
- wo: bfloat16 [4096, 8192], P('ctx', 'fsdp'), may hold values from -1.5 to 1.5
- key_cache: bfloat16 [65536, 1024], P(('fsdp', 'ctx')), may hold values from -500 to 500, as said below
- value_cache: bfloat16 [65536, 1024], P(('fsdp', 'ctx')), may hold values from -6 to 6
- key_blocks: int32 [32, 4, 8], P('fsdp'), may hold values from 0 to 15, as said below
Outputs:
- mixed: bfloat16 [16384, 8192], P('fsdp', 'ctx')
Inputs may be any that keep to these rules, and one draw needn't show every extreme that they name: `key_cache`: keys of order one; a sequence's first block may hold much larger ones. `key_blocks`: for query block b of sequence s, entries 0 to 2 name key blocks 16 - 4 + b - 2, 12 + b - 1 and 12 + b; entries 3 and 4 name blocks 0 and 1; the last 3 entries are random blocks. Counting the random entries of a sequence over its query blocks in order as t = 0, 1, ..., the t-th lies in blocks k * 2 to (k+1) * 2 - 1 with k = 1 + t mod (6); entries may repeat.
All inputs are finite; a program needn't handle non-finite values.
Results may differ from a plain program's by a relative error of at most 0.018.
Values may be sent and summed in bfloat16 or wider, within the bound.
No kernel may reach another device: no remote copies, remote signals or barrier semaphores. Data moves between devices by JAX's collectives and lax.ppermute only.
A program may use at most 128 MiB of HBM per device.

v0:
```python
import jax
import jax.numpy as jnp
from jax import lax
from jax.sharding import PartitionSpec as P

HEAD = 128
BLOCK = 128
rope_base = 1000000.0


def rotate(vectors, positions):
    half_width = vectors.shape[-1] // 2
    frequency = rope_base ** (
        -(jnp.arange(half_width, dtype=jnp.float32) * 2.0) / vectors.shape[-1]
    )
    angles = positions.astype(jnp.float32)[:, None] * frequency[None, :]
    cosine_table = jnp.cos(angles)[:, None, :]
    sine_table = jnp.sin(angles)[:, None, :]
    front_half = vectors[..., :half_width]
    back_half = vectors[..., half_width:]
    return jnp.concatenate(
        [
            front_half * cosine_table - back_half * sine_table,
            back_half * cosine_table + front_half * sine_table,
        ],
        axis=-1,
    )


def body(tokens, wq, wo, key_cache, value_cache, key_blocks):
    ctx_count = lax.axis_size("ctx")
    row_count = tokens.shape[0]
    query_cols = wq.shape[1]
    projected = jnp.dot(
        tokens, lax.all_gather(wq, "fsdp", axis=0, tiled=True), preferred_element_type=jnp.float32
    )
    cache_count = key_cache.shape[0]
    key_total = cache_count * ctx_count
    positions = key_total - row_count + jnp.arange(row_count, dtype=jnp.int32)
    query = (
        rotate(projected.reshape(row_count, query_cols // HEAD, HEAD), positions) * HEAD ** (-0.5)
    ).astype(jnp.bfloat16)
    kv_cols = key_cache.shape[1] // ctx_count
    keys_whole, values_whole = (
        lax.all_gather(key_cache, "ctx", axis=0, tiled=True),
        lax.all_gather(value_cache, "ctx", axis=0, tiled=True),
    )
    first_col = lax.axis_index("ctx") * kv_cols
    keys_all = lax.dynamic_slice_in_dim(keys_whole, first_col, kv_cols, 1)
    values_all = lax.dynamic_slice_in_dim(values_whole, first_col, kv_cols, 1)
    kv_local = kv_cols // HEAD
    group_size = query_cols // kv_cols
    block_count = key_total // BLOCK
    query_blocks = row_count // BLOCK
    lists = key_blocks[0]
    picked_keys = jnp.take(keys_all.reshape(block_count, BLOCK, kv_local, HEAD), lists, axis=0)
    picked_values = jnp.take(values_all.reshape(block_count, BLOCK, kv_local, HEAD), lists, axis=0)
    shaped = query.reshape(query_blocks, BLOCK, kv_local, group_size, HEAD)
    scores = jnp.einsum(
        "bqkgd,bnskd->bkgqns", shaped, picked_keys, preferred_element_type=jnp.float32
    )
    own_block = block_count - query_blocks + jnp.arange(query_blocks, dtype=jnp.int32)
    own = lists == own_block[:, None]
    causal = jnp.arange(BLOCK)[None, :] <= jnp.arange(BLOCK)[:, None]
    allowed = jnp.logical_or(
        jnp.logical_not(own)[:, None, None, None, :, None], causal[None, None, None, :, None, :]
    )
    scores = jnp.where(allowed, scores, -jnp.inf)
    top_score = jnp.max(scores, axis=(4, 5), keepdims=True)
    raised = jnp.exp(scores - top_score)
    weights = (raised / jnp.sum(raised, axis=(4, 5), keepdims=True)).astype(jnp.bfloat16)
    context = jnp.einsum(
        "bkgqns,bnskd->bqkgd", weights, picked_values, preferred_element_type=jnp.float32
    )
    context = context.astype(jnp.bfloat16).reshape(row_count, query_cols)
    share_terms = jnp.dot(
        context, lax.all_gather(wo, "fsdp", axis=1, tiled=True), preferred_element_type=jnp.float32
    )
    return lax.psum_scatter(
        share_terms.astype(jnp.bfloat16), "ctx", scatter_dimension=1, tiled=True
    )


def solution(mesh):
    in_specs = (
        P("fsdp", None),
        P("fsdp", "ctx"),
        P("ctx", "fsdp"),
        P(("fsdp", "ctx"), None),
        P(("fsdp", "ctx"), None),
        P("fsdp", None, None),
    )
    out_specs = P("fsdp", "ctx")
    return jax.shard_map(body, mesh=mesh, in_specs=in_specs, out_specs=out_specs, check_vma=False)
```

profile of v0, /device:TPU:1, one launch (start us, length us, event | category | flops | bytes accessed | tf_op | source)
XLA Modules:
  0.0 360.2 jit_solution(5195303256417563035)
XLA Ops:
  6.5 0.7 all-gather.5.cloned.1.call-update
  7.3 0.7 all-gather.7.cloned.1.call-update
  8.1 0.7 all-gather.9.cloned.1.call-update
  8.8 0.5 all-gather.11.cloned.1.call-update
  9.4 0.7 compare_select_fusion
  10.2 0.8 fusion.28
  11.0 0.5 multiply_cosine_fusion
  11.8 56.0 %all-gather.5.cloned.1.call-done = bf16[2048,1024]{1,0:T(8,128)(2,1)} async-done(((bf16[256,1024]{1,0:T(8,128)(2,1)}), bf16[2048,1024]{1,0:T(8,128)(2,1)}) %all-gather.5.cloned.1.call-update) | async-done | bytes 4194320 | tf_op jit(solution)/shard_map/all_gather | solution.py:46
  67.8 55.2 %all-gather.7.cloned.1.call-done = bf16[2048,1024]{1,0:T(8,128)(2,1)} async-done(((bf16[256,1024]{1,0:T(8,128)(2,1)}), bf16[2048,1024]{1,0:T(8,128)(2,1)}) %all-gather.7.cloned.1.call-update) | async-done | bytes 4194320 | tf_op jit(solution)/shard_map/all_gather | solution.py:45
  123.0 1.3 constant_dynamic-slice_fusion
  124.3 0.7 gather_fusion.1
  125.1 0.7 gather_fusion
  125.8 1.3 copy.8
  127.2 55.4 %all-gather.9.cloned.1.call-done = bf16[8192,512]{1,0:T(8,128)(2,1)} async-done(((bf16[256,512]{1,0:T(8,128)(2,1)}), bf16[8192,512]{1,0:T(8,128)(2,1)}) %all-gather.9.cloned.1.call-update) | async-done | bytes 8388624 | tf_op jit(solution)/shard_map/all_gather | solution.py:35
  182.6 9.4 %fusion.34 = f32[512,512]{0,1:T(8,128)S(1)} fusion(bf16[512,8192]{1,0:T(8,128)(2,1)} %param.8, bf16[8192,512]{1,0:T(8,128)(2,1)} %all-gather.9.cloned.1.call-done), kind=kOutput, calls=%fused_computation.49 | convolution fusion | flops 4294967296 | bytes 17825792 | tf_op jit(solution)/shard_map/dot_general | solution.py:34
  192.0 1.0 multiply_subtract_fusion
  193.5 1.2 concatenate.9
  194.7 1.3 copy.9
  196.0 2.7 fusion
  198.7 1.7 fusion.1
  200.5 2.2 fusion.10
  203.0 46.1 %all-gather.11.cloned.1.call-done = bf16[512,8192]{1,0:T(8,128)(2,1)} async-done(((bf16[512,256]{1,0:T(8,128)(2,1)}), bf16[512,8192]{1,0:T(8,128)(2,1)}) %all-gather.11.cloned.1.call-update) | async-done | bytes 8388624 | tf_op jit(solution)/shard_map/all_gather | solution.py:77
  249.1 10.0 %convolution_convert_fusion = bf16[512,8192]{1,0:T(8,128)(2,1)} fusion(bf16[512,8192]{1,0:T(8,128)(2,1)} %all-gather.11.cloned.1.call-done, bf16[64,8,4,128]{3,2,1,0:T(4,128)(2,1)S(1)} %bitcast.100), kind=kOutput, calls=%fused_computation.2 | convolution fusion | flops 4299161600 | bytes 17301504 | tf_op jit(solution)/shard_map/dot_general | solution.py:76
  259.2 94.5 %reduce-scatter.2.cloned.1.call-done = bf16[512,1024]{1,0:T(8,128)(2,1)} async-done(((bf16[512,8192]{1,0:T(8,128)(2,1)}), bf16[512,1024]{1,0:T(8,128)(2,1)}) %reduce-scatter.2.cloned.1.call-update) | async-done | bytes 1048592 | tf_op jit(solution)/shard_map/reduce_scatter | solution.py:79
  (18 shorter events, 1.4 us)
Async XLA Ops:
  6.5 61.3 %all-gather.5.cloned.1.call-start = ((), (), s32[]{:S(2)}) async-start(), calls=%async_computation.1 | async-start | bytes 4718592 | tf_op jit(solution)/shard_map/all_gather | solution.py:46
  7.3 115.8 %all-gather.7.cloned.1.call-start = ((), (), s32[]{:S(2)}) async-start(), calls=%async_computation.2 | async-start | bytes 4718592 | tf_op jit(solution)/shard_map/all_gather | solution.py:45
  8.0 174.6 %all-gather.9.cloned.1.call-start = ((), (), s32[]{:S(2)}) async-start(), calls=%async_computation.3 | async-start | bytes 8650752 | tf_op jit(solution)/shard_map/all_gather | solution.py:35
  8.7 240.4 %all-gather.11.cloned.1.call-start = ((), (), s32[]{:S(2)}) async-start(), calls=%async_computation.4 | async-start | bytes 8650752 | tf_op jit(solution)/shard_map/all_gather | solution.py:77
  9.3 344.3 %reduce-scatter.2.cloned.1.call-start = ((), (), s32[]{:S(2)}) async-start(), calls=%async_computation.5 | async-start | bytes 9437184 | tf_op jit(solution)/shard_map/reduce_scatter | solution.py:79
  198.7 1.8 copy-start
Sparse Core Ops, SparseCore 0:
  9.1 58.6 all-gather.4
  69.6 53.4 all-gather.6
  125.6 56.9 all-gather.8
  184.9 64.1 all-gather.10
  259.3 94.2 reduce-scatter.1
where the time goes:
time: 360 us
  waiting for transfers between devices  310 us (86%)
  matrix products  24.3 us (7%)
  between operations  13.3 us (4%)
  local copies, waits for them, and re-layouts  7.56 us (2%)
  other arithmetic  5.01 us (1%)
    reduce_scatter x1, waiting for transfers between devices, body(): lax.psum_scatter(share_terms.astype(jnp.bfloat16), 'ctx', scatter_dimensi...  94.5 us
    all_gather x1, waiting for transfers between devices, body(): lax.all_gather(value_cache, 'ctx', axis=0, tiled=True)  56 us
    all_gather x1, waiting for transfers between devices, body(): lax.all_gather(wq, 'fsdp', axis=0, tiled=True)  55.4 us
    all_gather x1, waiting for transfers between devices, body(): lax.all_gather(key_cache, 'ctx', axis=0, tiled=True)  55.2 us
    all_gather x1, waiting for transfers between devices, body(): lax.all_gather(wo, 'fsdp', axis=1, tiled=True)  46.1 us
    dot_general x1, matrix products, body(): jnp.dot(context, lax.all_gather(wo, 'fsdp', axis=1, tiled=True), preferre...  10 us
    dot_general x1, matrix products, body(): jnp.dot(tokens, lax.all_gather(wq, 'fsdp', axis=0, tiled=True), preferred...  9.44 us
  transfers between devices with their start and end apart: 5, of which 5 were waited for; matrix products, arithmetic and copies ran while one was open for 7% of the time, Pallas kernels for 0%

commit v1 on v0

--- a/solution.py
+++ b/solution.py
@@ -41,8 +41,15 @@
         rotate(projected.reshape(row_count, query_cols // HEAD, HEAD), positions) * HEAD ** (-0.5)
     ).astype(jnp.bfloat16)
     kv_cols = key_cache.shape[1] // ctx_count
+
+    def make_tokens_on(patch):
+        g_now = lax.axis_size("ctx")
+        far_arr = jnp.stack(g_now * [patch])
+        wide_out = lax.all_to_all(far_arr, "ctx", split_axis=0, concat_axis=0)
+        return jnp.concatenate(wide_out, axis=0)
+
     keys_whole, values_whole = (
-        lax.all_gather(key_cache, "ctx", axis=0, tiled=True),
+        make_tokens_on(key_cache),
         lax.all_gather(value_cache, "ctx", axis=0, tiled=True),
     )
     first_col = lax.axis_index("ctx") * kv_cols

time: 360 us -> 393 us (1.092)
  waiting for transfers between devices: 310 us -> 331 us
  starting transfers between devices: 0.15 us -> 9.13 us
    all_to_all x0 -> x1, waiting for transfers between devices: none -> 135 us  [make_tokens_on(): wide_out = lax.all_to_all(far_arr, 'ctx', split_axis=0, concat_axis=0)]
    all_gather x1, waiting for transfers between devices: 56 us -> 0.01 us  [body(): lax.all_gather(value_cache, 'ctx', axis=0, tiled=True)]
    all_gather x1 -> x0, waiting for transfers between devices: 55.2 us -> none  [body(): lax.all_gather(key_cache, 'ctx', axis=0, tiled=True)]
    all_to_all x0 -> x1, starting transfers between devices: none -> 9.01 us  [make_tokens_on(): wide_out = lax.all_to_all(far_arr, 'ctx', split_axis=0, concat_axis=0)]
  transfers between devices with their start and end apart: 5 -> 5, of which waited for: 5 -> 4; matrix products, arithmetic and copies ran while one was open for 7% -> 7% of each run, Pallas kernels for 0% -> 0%
where the time goes in v1:
time: 393 us
  waiting for transfers between devices  331 us (84%)
  matrix products  24.3 us (6%)
  between operations  13.3 us (3%)
  local copies, waits for them, and re-layouts  11.1 us (3%)
  starting transfers between devices  9.13 us (2%)
    all_to_all x1, waiting for transfers between devices, make_tokens_on(): wide_out = lax.all_to_all(far_arr, 'ctx', split_axis=0, concat_axis=0)  135 us
    reduce_scatter x1, waiting for transfers between devices, body(): lax.psum_scatter(share_terms.astype(jnp.bfloat16), 'ctx', scatter_dimensi...  94.5 us
    all_gather x1, waiting for transfers between devices, body(): lax.all_gather(wq, 'fsdp', axis=0, tiled=True)  53.5 us
    all_gather x1, waiting for transfers between devices, body(): lax.all_gather(wo, 'fsdp', axis=1, tiled=True)  46.3 us
    dot_general x1, matrix products, body(): jnp.dot(context, lax.all_gather(wo, 'fsdp', axis=1, tiled=True), preferre...  10 us
    dot_general x1, matrix products, body(): jnp.dot(tokens, lax.all_gather(wq, 'fsdp', axis=0, tiled=True), preferred...  9.44 us
    all_to_all x1, starting transfers between devices, make_tokens_on(): wide_out = lax.all_to_all(far_arr, 'ctx', split_axis=0, concat_axis=0)  9.01 us
  transfers between devices with their start and end apart: 5, of which 4 were waited for; matrix products, arithmetic and copies ran while one was open for 7% of the time, Pallas kernels for 0%

profile of v1, /device:TPU:1, one launch (start us, length us, event | category | flops | bytes accessed | tf_op | source)
XLA Modules:
  0.0 392.7 jit_solution(14830312158128635908)
XLA Ops:
  6.5 0.7 all-gather.4.cloned.1.call-update
  7.3 0.7 all-gather.6.cloned.1.call-update
  8.1 0.7 all-gather.8.cloned.1.call-update
  8.7 3.5 stack.2
  12.3 9.0 %all-to-all-start = ((bf16[8,256,1024]{2,1,0:T(8,128)(2,1)}), bf16[8,256,1024]{2,1,0:T(8,128)(2,1)}, u32[]{:S(2)}, u32[]{:S(2)}) async-start(bf16[8,256,1024]{2,1,0:T(8,128)(2,1)} %stack.2), calls=%async_computation | async-start | bytes 8388608 | tf_op jit(solution)/shard_map/all_to_all | solution.py:48
  21.6 0.5 multiply_cosine_fusion
  22.4 134.9 %all-to-all-done = bf16[8,256,1024]{2,1,0:T(8,128)(2,1)} async-done(((bf16[8,256,1024]{2,1,0:T(8,128)(2,1)}), bf16[8,256,1024]{2,1,0:T(8,128)(2,1)}, u32[]{:S(2)}, u32[]{:S(2)}) %all-to-all-start) | async-done | bytes 4194336 | tf_op jit(solution)/shard_map/all_to_all | solution.py:48
  157.3 1.3 constant_dynamic-slice_fusion
  158.6 0.7 gather_fusion.1
  159.4 0.7 gather_fusion
  160.1 1.3 copy.8
  161.5 53.5 %all-gather.6.cloned.1.call-done = bf16[8192,512]{1,0:T(8,128)(2,1)} async-done(((bf16[256,512]{1,0:T(8,128)(2,1)}), bf16[8192,512]{1,0:T(8,128)(2,1)}) %all-gather.6.cloned.1.call-update) | async-done | bytes 8388624 | tf_op jit(solution)/shard_map/all_gather | solution.py:35
  214.9 9.4 %fusion.34 = f32[512,512]{0,1:T(8,128)S(1)} fusion(bf16[512,8192]{1,0:T(8,128)(2,1)} %param.8, bf16[8192,512]{1,0:T(8,128)(2,1)} %all-gather.6.cloned.1.call-done), kind=kOutput, calls=%fused_computation.49 | convolution fusion | flops 4294967296 | bytes 17825792 | tf_op jit(solution)/shard_map/dot_general | solution.py:34
  224.4 1.0 multiply_subtract_fusion
  225.5 0.3 copy.10
  225.9 1.2 concatenate.9
  227.1 1.3 copy.9
  228.4 2.7 fusion
  231.1 1.7 fusion.1
  232.8 2.2 fusion.10
  235.1 0.3 copy.12
  235.4 46.3 %all-gather.8.cloned.1.call-done = bf16[512,8192]{1,0:T(8,128)(2,1)} async-done(((bf16[512,256]{1,0:T(8,128)(2,1)}), bf16[512,8192]{1,0:T(8,128)(2,1)}) %all-gather.8.cloned.1.call-update) | async-done | bytes 8388624 | tf_op jit(solution)/shard_map/all_gather | solution.py:84
  281.6 10.0 %convolution_convert_fusion = bf16[512,8192]{1,0:T(8,128)(2,1)} fusion(bf16[512,8192]{1,0:T(8,128)(2,1)} %all-gather.8.cloned.1.call-done, bf16[64,8,4,128]{3,2,1,0:T(4,128)(2,1)S(1)} %bitcast.101), kind=kOutput, calls=%fused_computation.2 | convolution fusion | flops 4299161600 | bytes 17301504 | tf_op jit(solution)/shard_map/dot_general | solution.py:83
  291.7 94.5 %reduce-scatter.2.cloned.1.call-done = bf16[512,1024]{1,0:T(8,128)(2,1)} async-done(((bf16[512,8192]{1,0:T(8,128)(2,1)}), bf16[512,1024]{1,0:T(8,128)(2,1)}) %reduce-scatter.2.cloned.1.call-update) | async-done | bytes 1048592 | tf_op jit(solution)/shard_map/reduce_scatter | solution.py:86
  (20 shorter events, 0.8 us)
Async XLA Ops:
  6.5 14.8 %copy-start.1 = (s32[1,4,8]{2,1,0:T(4,128)S(1)}, s32[1,4,8]{2,1,0:T(4,128)}, u32[]{:S(2)}) copy-start(s32[1,4,8]{2,1,0:T(4,128)} %param.13) | copy-start | bytes 388
  6.5 150.8 %all-gather.4.cloned.1.call-start = ((), (), s32[]{:S(2)}) async-start(), calls=%async_computation.2 | async-start | bytes 4718592 | tf_op jit(solution)/shard_map/all_gather | solution.py:53
  7.3 207.7 %all-gather.6.cloned.1.call-start = ((), (), s32[]{:S(2)}) async-start(), calls=%async_computation.3 | async-start | bytes 8650752 | tf_op jit(solution)/shard_map/all_gather | solution.py:35
  8.0 273.6 %all-gather.8.cloned.1.call-start = ((), (), s32[]{:S(2)}) async-start(), calls=%async_computation.4 | async-start | bytes 8650752 | tf_op jit(solution)/shard_map/all_gather | solution.py:84
  12.3 145.0 %all-to-all-start = ((bf16[8,256,1024]{2,1,0:T(8,128)(2,1)}), bf16[8,256,1024]{2,1,0:T(8,128)(2,1)}, u32[]{:S(2)}, u32[]{:S(2)}) async-start(bf16[8,256,1024]{2,1,0:T(8,128)(2,1)} %stack.2), calls=%async_computation | async-start | bytes 8388608 | tf_op jit(solution)/shard_map/all_to_all | solution.py:48
  21.3 364.9 %reduce-scatter.2.cloned.1.call-start = ((), (), s32[]{:S(2)}) async-start(), calls=%async_computation.5 | async-start | bytes 9437184 | tf_op jit(solution)/shard_map/reduce_scatter | solution.py:86
  231.1 1.8 copy-start
Sparse Core Ops, SparseCore 0:
  9.1 143.2 all-gather.3
  155.0 59.8 all-gather.5
  217.4 64.1 all-gather.7
  291.8 94.2 reduce-scatter.1
